TPU v7x, 32 devices: a whole 2x2x4 slice. The times are simulated.
32 devices in a mesh: groups: 2 (over x), seq: 16 (over z, y, core).
Axes of the slice: x: 2, y: 2, z: 4, core: 2. Of those that a mesh axis runs over, the one named last changes fastest.
Arguments:
- queries: bfloat16 [4096, 2048], P(('groups', 'seq')), parts along dimension 0, may hold values from -6 to 6
- keys: bfloat16 [4096, 1024], P(('groups', 'seq')), parts along dimension 0, may hold values from -6 to 6
- target_rows: bfloat16 [512, 2048], replicated, may hold values from -6 to 6
- target_ids: int32 [4096, 4], P(('groups', 'seq')), parts along dimension 0, may hold values from 0 to 511
- target_weight: float32 [4096, 4], P(('groups', 'seq')), parts along dimension 0, may hold values from -3 to 3
- block_mask: int32 [32, 7], P(('groups', 'seq')), parts along dimension 0, may hold values 0 or 1
- value_table: bfloat16 [1024, 1024], P('seq'), may hold values from -0.75 to 0.75
- feat_shard: int32 [4096, 8], P(('groups', 'seq')), parts along dimension 0, may hold values from 0 to 15, all different within a row; in each aligned block of 128 rows (0 to 127, 128 to 255, ...) at most 96 rows name the same one
- feat_row: int32 [4096, 8], P(('groups', 'seq')), parts along dimension 0, may hold values from 0 to 63
- activation: float32 [4096, 8], P(('groups', 'seq')), parts along dimension 0, may hold values from 0.2 to 5
- counts: int32 [4096], P(('groups', 'seq')), parts along dimension 0, may hold values from 1 to 8, 12288 in all
Outputs:
- value_grad: bfloat16 [4096, 1024], P(('groups', 'seq')), parts along dimension 0
- edges: float32 [4096, 8], P(('groups', 'seq')), parts along dimension 0
There are 2 independent parts, one for each index of `groups`. A program takes and returns all parts, laid end to end along the dimension named above; an argument that names none is the same for every part. Nothing has to cross between parts.
Inputs may be any that keep to these rules, and one draw needn't show every extreme that they name: `feat_shard`: the 8 shards named by one token are different; among the tokens of one block no shard is named by more than 96 slots, a bound that some block reaches. The counts of a prompt sum to 12288.
All inputs are finite; a program needn't handle non-finite values. No bound on the sum of `block_mask` or of `counts` on one device may be relied on, other than what follows from the above.
Results may differ from a plain program's by a relative error of at most 0.0085.
Values may be sent and summed in bfloat16 or wider, within the bound.
A program may use at most 128 MiB of HBM per device.

v0:
```python
import jax
import jax.numpy as jnp
from jax import lax
from jax.sharding import PartitionSpec as P

H = 16
KVH = 8
HD = 128
QPRE = 144
WB = 8
FEAT_DEV = 64


SOFTCAP = 50.0


def shifted(block, axis, distance):
    devices = range(lax.axis_size(axis))
    route = [(i - distance, i) for i in devices if i - distance in devices]
    return lax.ppermute(block, axis, route)


def tile_logits(query, kblock):
    scores = jnp.einsum(
        "qhgd,khd->hgqk", query, kblock, preferred_element_type=jnp.float32
    ) * QPRE ** (-0.5)
    return SOFTCAP * jnp.tanh(scores / SOFTCAP)


def body(
    queries,
    keys,
    target_rows,
    target_ids,
    target_weight,
    block_mask,
    value_table,
    feat_shard,
    feat_row,
    activation,
    counts,
):
    tok_rows = queries.shape[0]
    kv_width = keys.shape[1]
    head_group = H // KVH
    active_slots = feat_shard.shape[1]
    position = lax.axis_index("seq")
    head_grad = jnp.sum(
        target_weight[:, :, None] * target_rows[target_ids].astype(jnp.float32), axis=1
    ).astype(jnp.bfloat16)
    head_grads = head_grad.reshape(tok_rows, KVH, head_group, HD)
    query = queries.reshape(tok_rows, KVH, head_group, HD)
    lower_tri = jnp.arange(tok_rows)[:, None] >= jnp.arange(tok_rows)[None, :]
    blocks = [keys]
    for distance in range(1, WB):
        blocks.append(shifted(keys, "seq", distance))
    allowed = [None] + [
        (block_mask[0, distance - 1] == 1) & (position >= distance) for distance in range(1, WB)
    ]

    def expo(kblock, diagonal):
        weights = jnp.exp(tile_logits(query, kblock.reshape(tok_rows, KVH, HD)))
        if diagonal:
            weights = jnp.where(lower_tri[None, None], weights, 0.0)
        return weights

    tiles = [expo(blocks[0], True)]
    for distance in range(1, WB):
        tiles.append(
            lax.cond(
                allowed[distance],
                lambda kblock: expo(kblock, False),
                lambda kblock: jnp.zeros_like(tiles[0]),
                blocks[distance],
            )
        )
    totals = jnp.sum(tiles[0], axis=-1)
    for distance in range(1, WB):
        totals = totals + jnp.sum(tiles[distance], axis=-1)

    def partial_grad(weights):
        pattern = (weights / totals[..., None]).astype(jnp.bfloat16)
        return jnp.einsum(
            "hgqk,qhgd->khd", pattern, head_grads, preferred_element_type=jnp.float32
        ).reshape(tok_rows, kv_width)

    partials = [partial_grad(tiles[0])]
    for distance in range(1, WB):
        partials.append(
            lax.cond(
                allowed[distance],
                partial_grad,
                lambda weights: jnp.zeros((tok_rows, kv_width), jnp.float32),
                tiles[distance],
            )
        )
    summed = partials[0]
    for distance in range(1, WB):
        summed = summed + shifted(partials[distance], "seq", -distance)
    value_grad = summed.astype(jnp.bfloat16)
    live = jnp.arange(active_slots)[None, :] < counts[:, None]
    feature = feat_shard * FEAT_DEV + feat_row
    piece = lax.all_gather(value_table, "seq", axis=0, tiled=True)
    product = lax.dot_general(
        value_grad, piece, (((1,), (1,)), ((), ())), preferred_element_type=jnp.float32
    )
    extent = piece.shape[0]
    inside = (feature >= 0) & (feature < extent)
    values = jnp.take_along_axis(product, jnp.clip(feature, 0, extent - 1), axis=1)
    raw = jnp.where(inside, values, 0.0)
    edges = jnp.where(live, activation * raw, 0.0)
    return (value_grad, edges)


def solution(mesh):
    in_specs = (
        P(("groups", "seq"), None),
        P(("groups", "seq"), None),
        P(),
        P(("groups", "seq"), None),
        P(("groups", "seq"), None),
        P(("groups", "seq"), None),
        P("seq", None),
        P(("groups", "seq"), None),
        P(("groups", "seq"), None),
        P(("groups", "seq"), None),
        P(("groups", "seq")),
    )
    out_specs = (P(("groups", "seq"), None), P(("groups", "seq"), None))
    return jax.shard_map(body, mesh=mesh, in_specs=in_specs, out_specs=out_specs, check_vma=False)
```

profile of v0, /device:TPU:4, one launch (start us, length us, event | category | flops | bytes accessed | tf_op | source)
XLA Modules:
  0.0 215.4 jit_solution(4888012120594266005)
XLA Ops:
  7.9 4.6 %collective-permute-start.6 = (bf16[128,1024]{1,0:T(8,128)(2,1)}, bf16[128,1024]{1,0:T(8,128)(2,1)}, u32[]{:S(2)}, u32[]{:S(2)}) collective-permute-start(bf16[128,1024]{1,0:T(8,128)(2,1)} %param.40), channel_id=1, source_target_pairs={{0,7},{1,8},{2,9},{3,10},{4,11},{5,12},{6,13},{7,14},{8,15},{16,23... | collective-permute-start | bytes 786440 | tf_op jit(solution)/shard_map/ppermute | solution.py:20
  12.5 4.4 %collective-permute-start.5 = (bf16[128,1024]{1,0:T(8,128)(2,1)}, bf16[128,1024]{1,0:T(8,128)(2,1)}, u32[]{:S(2)}, u32[]{:S(2)}) collective-permute-start(bf16[128,1024]{1,0:T(8,128)(2,1)} %param.40), channel_id=1, source_target_pairs={{0,6},{1,7},{2,8},{3,9},{4,10},{5,11},{6,12},{7,13},{8,14},{9,15},... | collective-permute-start | bytes 786440 | tf_op jit(solution)/shard_map/ppermute | solution.py:20
  16.9 2.0 collective-permute-start.4
  18.9 2.0 collective-permute-start.3
  20.9 2.0 collective-permute-start.2
  23.8 3.4 %gather_fusion = bf16[512,2048]{1,0:T(8,128)(2,1)} fusion(bf16[512,2048]{1,0:T(8,128)(2,1)S(1)} %copy-done, s32[1024]{0:T(1024)S(1)} %pad_clamp_fusion), kind=kCustom, calls=%fused_computation | custom fusion | bytes 4196352 | tf_op jit(solution)/shard_map/gather | solution.py:49
  27.2 4.7 %reshape.144 = f32[128,4,2048]{2,1,0:T(4,128)} reshape(bf16[512,2048]{1,0:T(8,128)(2,1)} %gather_fusion) | data formatting | bytes 6291456 | tf_op jit(solution)/shard_map/convert_element_type | solution.py:49
  32.1 5.5 %multiply_reduce_fusion = bf16[128,2048]{1,0:T(8,128)(2,1)S(1)} fusion(f32[128,4,2048]{2,1,0:T(4,128)} %reshape.144, f32[128,4]{1,0:T(8,128)S(1)} %copy.135), kind=kLoop, calls=%fused_computation.65 | loop fusion | flops 1835008 | bytes 4720640 | tf_op jit(solution)/shard_map/reduce_sum | solution.py:48
  44.8 2.1 collective-permute-start.1
  46.9 1.9 collective-permute-start
  48.8 2.5 %fusion.72 = (f32[8,2,128]{2,1,0:T(2,128)S(1)}, f32[8,2,128,128]{2,3,1,0:T(8,128)}) fusion(bf16[128,8,2,128]{0,3,2,1:T(8,128)(2,1)} %bitcast.161, bf16[128,8,128,1]{2,1,0,3:T(8,128)(2,1)S(1)} %bitcast.171, pred[128,128]{0,1:T(8,128)(4,1)S(1)} %iota_compare_fusion), kind=kOutput, calls=%fused_computation.102 | convolution fusion | flops 68155392 | bytes 1859584 | tf_op jit(solution)/shard_map/qhgd,khd->hgqk/dot_general | solution.py:24
  52.0 1.7 conditional.19
  53.7 1.8 conditional.18
  57.2 1.7 conditional.16
  59.4 1.7 conditional.15
  61.1 1.7 conditional.14
  64.5 2.0 copy.161
  68.7 2.1 copy.164
  72.9 2.1 copy.151
  75.0 11.0 %collective-permute-start.7 = (f32[128,1024]{1,0:T(8,128)}, f32[128,1024]{1,0:T(8,128)}, u32[]{:S(2)}, u32[]{:S(2)}) collective-permute-start(f32[128,1024]{1,0:T(8,128)} %copy.151), channel_id=1, source_target_pairs={{1,0},{2,1},{3,2},{4,3},{5,4},{6,5},{7,6},{8,7},{9,8},{10,9},{11,1... | collective-permute-start | bytes 1572872 | tf_op jit(solution)/shard_map/ppermute | solution.py:20
  86.8 2.0 copy.155
  88.9 1.9 collective-permute-start.8
  91.6 2.0 copy.158
  95.8 2.1 copy.167
  100.2 14.1 %collective-permute-done.11 = f32[128,1024]{1,0:T(8,128)} collective-permute-done((f32[128,1024]{1,0:T(8,128)}, f32[128,1024]{1,0:T(8,128)}, u32[]{:S(2)}, u32[]{:S(2)}) %collective-permute-start.11) | collective-permute-done | bytes 524320 | tf_op jit(solution)/shard_map/ppermute | solution.py:20
  115.9 2.5 %fusion.54 = f32[8,128,128,1]{2,1,3,0:T(8,128)} fusion(bf16[128,8,2,128]{3,2,1,0:T(2,128)(2,1)} %convert_element_type.67, f32[8,2,128,128]{2,3,1,0:T(8,128)} %get-tuple-element.343, f32[8,2,128]{2,1,0:T(2,128)S(1)} %fusion.63), kind=kOutput, calls=%fused_computation.73 | convolution fusion | flops 67633152 | bytes 2105344 | tf_op jit(solution)/shard_map/hgqk,qhgd->khd/dot_general | solution.py:83
  119.7 11.0 %collective-permute-done.9 = f32[128,1024]{1,0:T(8,128)} collective-permute-done((f32[128,1024]{1,0:T(8,128)}, f32[128,1024]{1,0:T(8,128)}, u32[]{:S(2)}, u32[]{:S(2)}) %collective-permute-start.9) | collective-permute-done | bytes 524320 | tf_op jit(solution)/shard_map/ppermute | solution.py:20
  130.7 52.2 %collective-permute-done.12 = f32[128,1024]{1,0:T(8,128)} collective-permute-done((f32[128,1024]{1,0:T(8,128)}, f32[128,1024]{1,0:T(8,128)}, u32[]{:S(2)}, u32[]{:S(2)}) %collective-permute-start.12) | collective-permute-done | bytes 524320 | tf_op jit(solution)/shard_map/ppermute | solution.py:20
  182.9 11.4 %collective-permute-done.13 = f32[128,1024]{1,0:T(8,128)} collective-permute-done((f32[128,1024]{1,0:T(8,128)}, f32[128,1024]{1,0:T(8,128)}, u32[]{:S(2)}, u32[]{:S(2)}) %collective-permute-start.13) | collective-permute-done | bytes 524320 | tf_op jit(solution)/shard_map/ppermute | solution.py:20
  194.3 2.3 %add_convert_fusion = bf16[128,1024]{1,0:T(8,128)(2,1)S(1)} fusion(f32[128,1024]{1,0:T(8,128)} %collective-permute-done.13, f32[128,1024]{1,0:T(8,128)} %collective-permute-done.12, f32[128,1024]{1,0:T(8,128)} %collective-permute-done.11, f32[128,1024]{1,0:T(8,128)} %collective-permute-done.10, f32[128,1024]{1,0:T(8,128)} %collective-permute-done.9, ...), kind=kLoop, calls=%fused_computation.75 | loop fusion | flops 1048576 | bytes 4456448 | tf_op jit(solution)/shard_map/convert_element_type | solution.py:100
  196.7 2.5 %fusion.73 = f32[128,1024]{1,0:T(8,128)S(1)} fusion(bf16[128,1024]{1,0:T(8,128)(2,1)S(1)} %add_convert_fusion, bf16[1024,1024]{1,0:T(8,128)(2,1)} %all-gather.2.cloned.1.call-done), kind=kOutput, calls=%fused_computation.103 | convolution fusion | flops 268435456 | bytes 2883584 | tf_op jit(solution)/shard_map/dot_general | solution.py:104
  199.2 8.6 %gather_fusion.1 = f32[1024]{0:T(1024)S(1)} fusion(f32[128,1024]{1,0:T(8,128)S(1)} %fusion.73, s32[1024]{0:T(1024)S(1)} %reshape.136), kind=kCustom, calls=%fused_computation.1 | custom fusion | bytes 16384 | tf_op jit(solution)/shard_map/jit(take_along_axis)/gather | solution.py:109
  (97 shorter events, 39.4 us)
Async XLA Ops:
  7.2 16.7 %copy-start = (bf16[512,2048]{1,0:T(8,128)(2,1)S(1)}, bf16[512,2048]{1,0:T(8,128)(2,1)}, u32[]{:S(2)}) copy-start(bf16[512,2048]{1,0:T(8,128)(2,1)} %param.41) | copy-start | bytes 6291460
  7.2 189.5 %all-gather.2.cloned.1.call-start = ((), (), s32[]{:S(2)}) async-start(), calls=%async_computation | async-start | bytes 2228224 | tf_op jit(solution)/shard_map/all_gather | solution.py:103
  7.9 36.9 %collective-permute-start.6 = (bf16[128,1024]{1,0:T(8,128)(2,1)}, bf16[128,1024]{1,0:T(8,128)(2,1)}, u32[]{:S(2)}, u32[]{:S(2)}) collective-permute-start(bf16[128,1024]{1,0:T(8,128)(2,1)} %param.40), channel_id=1, source_target_pairs={{0,7},{1,8},{2,9},{3,10},{4,11},{5,12},{6,13},{7,14},{8,15},{16,23... | collective-permute-start | bytes 786440 | tf_op jit(solution)/shard_map/ppermute | solution.py:20
  12.5 34.4 %collective-permute-start.5 = (bf16[128,1024]{1,0:T(8,128)(2,1)}, bf16[128,1024]{1,0:T(8,128)(2,1)}, u32[]{:S(2)}, u32[]{:S(2)}) collective-permute-start(bf16[128,1024]{1,0:T(8,128)(2,1)} %param.40), channel_id=1, source_target_pairs={{0,6},{1,7},{2,8},{3,9},{4,10},{5,11},{6,12},{7,13},{8,14},{9,15},... | collective-permute-start | bytes 786440 | tf_op jit(solution)/shard_map/ppermute | solution.py:20
  16.9 36.8 %collective-permute-start.4 = (bf16[128,1024]{1,0:T(8,128)(2,1)}, bf16[128,1024]{1,0:T(8,128)(2,1)}, u32[]{:S(2)}, u32[]{:S(2)}) collective-permute-start(bf16[128,1024]{1,0:T(8,128)(2,1)} %param.40), channel_id=1, source_target_pairs={{0,5},{1,6},{2,7},{3,8},{4,9},{5,10},{6,11},{7,12},{8,13},{9,14},{... | collective-permute-start | bytes 786440 | tf_op jit(solution)/shard_map/ppermute | solution.py:20
  18.9 36.6 %collective-permute-start.3 = (bf16[128,1024]{1,0:T(8,128)(2,1)}, bf16[128,1024]{1,0:T(8,128)(2,1)}, u32[]{:S(2)}, u32[]{:S(2)}) collective-permute-start(bf16[128,1024]{1,0:T(8,128)(2,1)} %param.40), channel_id=1, source_target_pairs={{0,4},{1,5},{2,6},{3,7},{4,8},{5,9},{6,10},{7,11},{8,12},{9,13},{1... | collective-permute-start | bytes 786440 | tf_op jit(solution)/shard_map/ppermute | solution.py:20
  20.9 36.3 %collective-permute-start.2 = (bf16[128,1024]{1,0:T(8,128)(2,1)}, bf16[128,1024]{1,0:T(8,128)(2,1)}, u32[]{:S(2)}, u32[]{:S(2)}) collective-permute-start(bf16[128,1024]{1,0:T(8,128)(2,1)} %param.40), channel_id=1, source_target_pairs={{0,3},{1,4},{2,5},{3,6},{4,7},{5,8},{6,9},{7,10},{8,11},{9,12},{10... | collective-permute-start | bytes 786440 | tf_op jit(solution)/shard_map/ppermute | solution.py:20
  27.2 4.7 %copy-start.9 = (f32[128,4]{0,1:T(4,128)S(1)}, f32[128,4]{0,1:T(4,128)}, u32[]{:S(2)}) copy-start(f32[128,4]{0,1:T(4,128)} %param.43) | copy-start | bytes 6148
  32.1 5.5 %copy-start.5 = (s32[1,7]{1,0:T(1,128)S(1)}, s32[1,7]{1,0:T(1,128)}, u32[]{:S(2)}) copy-start(s32[1,7]{1,0:T(1,128)} %param.44) | copy-start | bytes 88
  32.1 6.8 %copy-start.2 = (bf16[128,2048]{1,0:T(8,128)(2,1)S(1)}, bf16[128,2048]{1,0:T(8,128)(2,1)}, u32[]{:S(2)}) copy-start(bf16[128,2048]{1,0:T(8,128)(2,1)} %param.39) | copy-start | bytes 1572868
  32.1 11.5 %copy-start.4 = (bf16[128,1024]{1,0:T(8,128)(2,1)S(1)}, bf16[128,1024]{1,0:T(8,128)(2,1)}, u32[]{:S(2)}) copy-start(bf16[128,1024]{1,0:T(8,128)(2,1)} %param.40) | copy-start | bytes 786436
  44.8 6.5 %copy-start.3 = (bf16[128,2048]{0,1:T(8,128)(2,1)S(1)}, bf16[128,2048]{0,1:T(8,128)(2,1)}, u32[]{:S(2)}) copy-start(bf16[128,2048]{0,1:T(8,128)(2,1)} %copy.137) | copy-start | bytes 1572868
  44.8 14.6 %collective-permute-start.1 = (bf16[128,1024]{1,0:T(8,128)(2,1)S(1)}, bf16[128,1024]{1,0:T(8,128)(2,1)}, u32[]{:S(2)}, u32[]{:S(2)}) collective-permute-start(bf16[128,1024]{1,0:T(8,128)(2,1)S(1)} %copy-done.4), channel_id=1, source_target_pairs={{0,2},{1,3},{2,4},{3,5},{4,6},{5,7},{6,8},{7,9},{8,10},{9,11},{10,... | collective-permute-start | bytes 786440 | tf_op jit(solution)/shard_map/ppermute | solution.py:20
  46.9 14.2 %collective-permute-start = (bf16[128,1024]{1,0:T(8,128)(2,1)S(1)}, bf16[128,1024]{1,0:T(8,128)(2,1)}, u32[]{:S(2)}, u32[]{:S(2)}) collective-permute-start(bf16[128,1024]{1,0:T(8,128)(2,1)S(1)} %copy-done.4), channel_id=1, source_target_pairs={{0,1},{1,2},{2,3},{3,4},{4,5},{5,6},{6,7},{7,8},{8,9},{9,10},{10,1... | collective-permute-start | bytes 786440 | tf_op jit(solution)/shard_map/ppermute | solution.py:20
  66.5 32.4 %collective-permute-start.10 = (f32[128,1024]{1,0:T(8,128)}, f32[128,1024]{1,0:T(8,128)}, u32[]{:S(2)}, u32[]{:S(2)}) collective-permute-start(f32[128,1024]{1,0:T(8,128)} %copy.161), channel_id=1, source_target_pairs={{4,0},{5,1},{6,2},{7,3},{8,4},{9,5},{10,6},{11,7},{12,8},{13,9},{1... | collective-permute-start | bytes 1572872 | tf_op jit(solution)/shard_map/ppermute | solution.py:20
  70.8 43.6 %collective-permute-start.11 = (f32[128,1024]{1,0:T(8,128)}, f32[128,1024]{1,0:T(8,128)}, u32[]{:S(2)}, u32[]{:S(2)}) collective-permute-start(f32[128,1024]{1,0:T(8,128)} %copy.164), channel_id=1, source_target_pairs={{5,0},{6,1},{7,2},{8,3},{9,4},{10,5},{11,6},{12,7},{13,8},{14,9},{... | collective-permute-start | bytes 1572872 | tf_op jit(solution)/shard_map/ppermute | solution.py:20
  75.0 44.7 %collective-permute-start.7 = (f32[128,1024]{1,0:T(8,128)}, f32[128,1024]{1,0:T(8,128)}, u32[]{:S(2)}, u32[]{:S(2)}) collective-permute-start(f32[128,1024]{1,0:T(8,128)} %copy.151), channel_id=1, source_target_pairs={{1,0},{2,1},{3,2},{4,3},{5,4},{6,5},{7,6},{8,7},{9,8},{10,9},{11,1... | collective-permute-start | bytes 1572872 | tf_op jit(solution)/shard_map/ppermute | solution.py:20
  88.9 30.8 %collective-permute-start.8 = (f32[128,1024]{1,0:T(8,128)}, f32[128,1024]{1,0:T(8,128)}, u32[]{:S(2)}, u32[]{:S(2)}) collective-permute-start(f32[128,1024]{1,0:T(8,128)} %copy.155), channel_id=1, source_target_pairs={{2,0},{3,1},{4,2},{5,3},{6,4},{7,5},{8,6},{9,7},{10,8},{11,9},{12,... | collective-permute-start | bytes 1572872 | tf_op jit(solution)/shard_map/ppermute | solution.py:20
  93.7 37.0 %collective-permute-start.9 = (f32[128,1024]{1,0:T(8,128)}, f32[128,1024]{1,0:T(8,128)}, u32[]{:S(2)}, u32[]{:S(2)}) collective-permute-start(f32[128,1024]{1,0:T(8,128)} %copy.158), channel_id=1, source_target_pairs={{3,0},{4,1},{5,2},{6,3},{7,4},{8,5},{9,6},{10,7},{11,8},{12,9},{13... | collective-permute-start | bytes 1572872 | tf_op jit(solution)/shard_map/ppermute | solution.py:20
  97.9 17.7 %copy-start.6 = (s32[128,8]{0,1:T(8,128)S(1)}, s32[128,8]{0,1:T(8,128)}, u32[]{:S(2)}) copy-start(s32[128,8]{0,1:T(8,128)} %param.47) | copy-start | bytes 12292
  97.9 17.7 %copy-start.7 = (s32[128,8]{0,1:T(8,128)S(1)}, s32[128,8]{0,1:T(8,128)}, u32[]{:S(2)}) copy-start(s32[128,8]{0,1:T(8,128)} %param.46) | copy-start | bytes 12292
  98.9 84.0 %collective-permute-start.12 = (f32[128,1024]{1,0:T(8,128)}, f32[128,1024]{1,0:T(8,128)}, u32[]{:S(2)}, u32[]{:S(2)}) collective-permute-start(f32[128,1024]{1,0:T(8,128)} %copy.167), channel_id=1, source_target_pairs={{6,0},{7,1},{8,2},{9,3},{10,4},{11,5},{12,6},{13,7},{14,8},{15,9},... | collective-permute-start | bytes 1572872 | tf_op jit(solution)/shard_map/ppermute | solution.py:20
  114.3 80.0 %collective-permute-start.13 = (f32[128,1024]{1,0:T(8,128)}, f32[128,1024]{1,0:T(8,128)}, u32[]{:S(2)}, u32[]{:S(2)}) collective-permute-start(f32[128,1024]{1,0:T(8,128)} %copy.170), channel_id=1, source_target_pairs={{7,0},{8,1},{9,2},{10,3},{11,4},{12,5},{13,6},{14,7},{15,8},{23,16... | collective-permute-start | bytes 1572872 | tf_op jit(solution)/shard_map/ppermute | solution.py:20
  196.6 11.2 %copy-start.1 = (bf16[128,1024]{1,0:T(8,128)(2,1)}, bf16[128,1024]{1,0:T(8,128)(2,1)S(1)}, u32[]{:S(2)}) copy-start(bf16[128,1024]{1,0:T(8,128)(2,1)S(1)} %add_convert_fusion) | copy-start | bytes 786436
  199.2 8.8 %copy-start.8 = (f32[128,8]{0,1:T(8,128)S(1)}, f32[128,8]{0,1:T(8,128)}, u32[]{:S(2)}) copy-start(f32[128,8]{0,1:T(8,128)} %param.48) | copy-start | bytes 12292
  199.2 8.8 %copy-start.10 = (s32[128]{0:T(128)S(1)}, s32[128]{0:T(128)}, u32[]{:S(2)}) copy-start(s32[128]{0:T(128)} %param.49) | copy-start | bytes 1540
Sparse Core Ops, SparseCore 0:
  10.2 49.5 all-gather.1
where the time goes:
time: 219 us; the launch traced here: 215 us
  waiting for transfers between devices  89.9 us (41%)
  local copies, waits for them, and re-layouts  50.9 us (23%)
  starting transfers between devices  38.3 us (17%)
  between operations  18.7 us (9%)
  other arithmetic  9.99 us (5%)
  matrix products  7.5 us (3%)
    ppermute x14, waiting for transfers between devices, shifted(): return lax.ppermute(block, axis, route)  89.2 us
    ppermute x14, starting transfers between devices, shifted(): return lax.ppermute(block, axis, route)  38.3 us
    cond x7, local copies, waits for them, and re-layouts, body(): lax.cond(allowed[distance], partial_grad, lambda weights: jnp.zeros((tok_...  13.3 us
    another operation x14, local copies, waits for them, and re-layouts  11.9 us
    gather x5, local copies, waits for them, and re-layouts, body(): jnp.take_along_axis(product, jnp.clip(feature, 0, extent - 1), axis=1)  8.91 us
    reduce_sum x1, other arithmetic, body(): jnp.sum(target_weight[:, :, None] * target_rows[target_ids].astype(jnp.fl...  5.47 us
    convert_element_type x1, local copies, waits for them, and re-layouts, body(): target_rows[target_ids].astype(jnp.float32)  4.74 us
  transfers between devices with their start and end apart: 15, of which 5 were waited for; matrix products, arithmetic and copies ran while one was open for 26% of the time, Pallas kernels for 0%

commit v1 on v0

v1 whole, which is shorter than its diff:
```python
import functools
import math

import jax
import jax.numpy as jnp
from jax import lax
from jax.experimental import pallas as pl
from jax.experimental.pallas import tpu as pltpu
from jax.sharding import PartitionSpec as P

H = 16
KVH = 8
HD = 128
QPRE = 144
WB = 8
FEAT_DEV = 64
SOFTCAP = 50.0

CHUNKS = 4
GROUP = H // KVH
HEADS = KVH // CHUNKS
REACH = (WB - 2) // 2
ROLES = WB
MESH = pl.DeviceIdType.MESH
VMEM_LIMIT = 48 * 1024 * 1024


def attention_kernel(
    n,
    q_hbm,
    k_ref,
    rows_hbm,
    ids_ref,
    weight_ref,
    mask_ref,
    out_ref,
    q_vm,
    rows_vm,
    kbuf,
    hgrad,
    wbuf,
    acc,
    pown,
    psend,
    psum,
    rsib,
    rgrad,
    load_sem,
    ksend,
    krecv,
    gsend,
    grecv,
):
    tok = k_ref.shape[0]
    width = k_ref.shape[1] // CHUNKS
    b = lax.axis_index("seq")
    core = lax.rem(b, 2)
    chip = lax.div(b, 2)
    chips = n // 2
    sib = b + 1 - 2 * core
    ahead = [chip + d < chips for d in range(1, REACH + 1)]
    behind = [chip >= d for d in range(1, REACH + 1)]
    last_ahead = chip + 4 * core < chips
    last_behind = chip >= 4 * (1 - core)
    last_key_to = b + 1 + 6 * core
    last_grad_to = b - 7 + 6 * core
    far = b - 7 + 14 * core
    has_far = jnp.logical_and(far >= 0, far < n)

    load_q = pltpu.make_async_copy(q_hbm, q_vm, load_sem.at[0])
    load_rows = pltpu.make_async_copy(rows_hbm, rows_vm, load_sem.at[1])
    load_rows.start()
    load_q.start()

    barrier = pltpu.get_barrier_semaphore()
    partners = [(sib, None), (far, has_far)]
    for d in range(1, REACH + 1):
        partners.append((b + 2 * d, ahead[d - 1]))
        partners.append((b - 2 * d, behind[d - 1]))

    def greet(device):
        pl.semaphore_signal(barrier, inc=1, device_id={"seq": device}, device_id_type=MESH)

    for device, cond in partners:
        if cond is None:
            greet(device)
        else:
            pl.when(cond)(functools.partial(greet, device))
    peers = 1
    for _, cond in partners[1:]:
        peers = peers + jnp.where(cond, 1, 0)
    pl.semaphore_wait(barrier, peers)

    def cols(k):
        return pl.ds(pl.multiple_of(k * width, width), width)

    def remote(src, dst, send, recv, device):
        return pltpu.make_async_remote_copy(
            src_ref=src,
            dst_ref=dst,
            send_sem=send,
            recv_sem=recv,
            device_id={"seq": device},
            device_id_type=MESH,
        )

    def key_direct(d, k, device):
        return remote(
            k_ref.at[:, cols(k)], kbuf.at[d - 1, k], ksend.at[d - 1, k], krecv.at[d - 1, k], device
        )

    def key_share(d, k):
        i = REACH + d - 1
        return remote(kbuf.at[d - 1, k], kbuf.at[i, k], ksend.at[i, k], krecv.at[i, k], sib)

    def key_last(k, device):
        i = 2 * REACH
        return remote(k_ref.at[:, cols(k)], kbuf.at[i, k], ksend.at[i, k], krecv.at[i, k], device)

    def grad_share(d, k):
        return remote(
            psend.at[d - 1, k], rsib.at[d - 1, k], gsend.at[d - 1, k], grecv.at[d - 1, k], sib
        )

    def grad_direct(d, k, device):
        i = REACH + d - 1
        return remote(psum.at[d - 1, k], rgrad.at[d - 1, k], gsend.at[i, k], grecv.at[i, k], device)

    def grad_last(k, device):
        i = 2 * REACH
        return remote(
            psend.at[REACH, k], rgrad.at[REACH, k], gsend.at[i, k], grecv.at[i, k], device
        )

    for k in range(CHUNKS):
        for d in range(1, REACH + 1):
            pl.when(ahead[d - 1])(lambda d=d, k=k: key_direct(d, k, b + 2 * d).start())
        pl.when(last_ahead)(lambda k=k: key_last(k, last_key_to).start())

    load_rows.wait()
    targets = rows_vm.shape[0]
    lane = lax.broadcasted_iota(jnp.int32, (tok, targets), 1)
    spread = jnp.zeros((tok, targets), jnp.float32)
    for j in range(ids_ref.shape[1]):
        spread = spread + jnp.where(lane == ids_ref[:, j : j + 1], weight_ref[:, j : j + 1], 0.0)
    high = spread.astype(jnp.bfloat16)
    low = (spread - high.astype(jnp.float32)).astype(jnp.bfloat16)
    for g in range(KVH):
        part = rows_vm[:, g * GROUP * HD : (g + 1) * GROUP * HD]
        grad = jnp.dot(high, part, preferred_element_type=jnp.float32) + jnp.dot(
            low, part, preferred_element_type=jnp.float32
        )
        grad = grad.astype(jnp.bfloat16)
        for h in range(GROUP):
            hgrad[g, h * tok : (h + 1) * tok, :] = grad[:, h * HD : (h + 1) * HD]
    load_q.wait()

    key_row = lax.broadcasted_iota(jnp.int32, (tok, GROUP * tok), 0)
    tok_col = lax.rem(lax.broadcasted_iota(jnp.int32, (tok, GROUP * tok), 1), tok)
    causal = key_row <= tok_col

    def tile_work(k):
        for gi in range(HEADS):
            mine = slice(gi * HD, (gi + 1) * HD)
            pair = GROUP * HD
            offset = pl.multiple_of(k * (HEADS * pair) + gi * pair, pair)
            q = q_vm[:, pl.ds(offset, pair)]
            q2 = jnp.concatenate([q[:, h * HD : (h + 1) * HD] for h in range(GROUP)], axis=0)
            total = jnp.zeros((1, GROUP * tok), jnp.float32)
            for r in range(ROLES):
                if r == 0:
                    start = pl.multiple_of(k * width + gi * HD, HD)
                    key = k_ref[:, pl.ds(start, HD)]
                    keep = causal
                else:
                    key = kbuf[r - 1, k, :, mine]
                    keep = mask_ref[r : r + 1, :] > 0.5
                score = lax.dot_general(
                    key, q2, (((1,), (1,)), ((), ())), preferred_element_type=jnp.float32
                )
                logit = (SOFTCAP * math.log2(math.e)) * jnp.tanh(
                    score * (QPRE ** (-0.5) / SOFTCAP)
                )
                w = jnp.exp2(jnp.where(keep, logit, -1.0e5))
                wbuf[r] = w
                total = total + jnp.sum(w, axis=0, keepdims=True)
            scale = 1.0 / total
            grad = hgrad[k * HEADS + gi]
            for r in range(ROLES):
                pattern = (wbuf[r] * scale).astype(jnp.bfloat16)
                part = jnp.dot(pattern, grad, preferred_element_type=jnp.float32)
                if r == 0:
                    acc[k, :, mine] = part
                elif r <= REACH:
                    pown[r - 1, k, :, mine] = part
                else:
                    psend[r - 1 - REACH, k, :, mine] = part.astype(jnp.bfloat16)

    def reduce_pair(k):
        for d in range(1, REACH + 1):

            def one(d=d):
                grad_share(d, k).wait_recv()
                both = pown[d - 1, k] + rsib[d - 1, k].astype(jnp.float32)
                psum[d - 1, k] = both.astype(jnp.bfloat16)
                grad_direct(d, k, b - 2 * d).start()

            pl.when(behind[d - 1])(one)

    def chunk(k, carry):
        for d in range(1, REACH + 1):

            def share(d=d):
                key_direct(d, k, sib).wait_recv()
                key_share(d, k).start()

            pl.when(behind[d - 1])(share)
        for d in range(1, REACH + 1):
            pl.when(behind[d - 1])(lambda d=d: key_share(d, k).wait_recv())
        pl.when(last_behind)(lambda: key_last(k, sib).wait_recv())
        tile_work(k)
        for d in range(1, REACH + 1):
            pl.when(behind[d - 1])(lambda d=d: grad_share(d, k).start())
        pl.when(last_behind)(lambda: grad_last(k, last_grad_to).start())
        pl.when(k > 0)(lambda: reduce_pair(k - 1))
        return carry

    lax.fori_loop(0, CHUNKS, chunk, 0)
    reduce_pair(CHUNKS - 1)

    def finish(k, carry):
        for d in range(1, REACH + 1):

            def add(d=d):
                grad_direct(d, k, sib).wait_recv()
                acc[k] += rgrad[d - 1, k].astype(jnp.float32)

            pl.when(ahead[d - 1])(add)

        def add_last():
            grad_last(k, sib).wait_recv()
            acc[k] += rgrad[REACH, k].astype(jnp.float32)

        pl.when(last_ahead)(add_last)
        out_ref[:, cols(k)] = acc[k].astype(out_ref.dtype)
        return carry

    lax.fori_loop(0, CHUNKS, finish, 0)

    def drain(k, carry):
        for d in range(1, REACH + 1):
            pl.when(ahead[d - 1])(lambda d=d: key_direct(d, k, sib).wait_send())

            def back(d=d):
                key_share(d, k).wait_send()
                grad_share(d, k).wait_send()
                grad_direct(d, k, sib).wait_send()

            pl.when(behind[d - 1])(back)
        pl.when(last_ahead)(lambda: key_last(k, sib).wait_send())
        pl.when(last_behind)(lambda: grad_last(k, sib).wait_send())
        return carry

    lax.fori_loop(0, CHUNKS, drain, 0)


def edges_kernel(vg_ref, table_ref, shard_ref, row_ref, act_ref, vg_out, edges_ref, wide):
    tok, slots = shard_ref.shape
    vg = vg_ref[...]
    vg_out[...] = vg
    wide[...] = jnp.zeros_like(wide)
    wide[:, 0:slots] = shard_ref[...] * FEAT_DEV + row_ref[...]
    feature = wide[...]
    tile = lax.div(feature, 128)
    within = lax.rem(feature, 128)
    step = 256

    def piece(i, found):
        rows = table_ref[pl.ds(pl.multiple_of(i * step, step), step), :]
        product = lax.dot_general(
            vg, rows, (((1,), (1,)), ((), ())), preferred_element_type=jnp.float32
        )
        for j in range(step // 128):
            picked = jnp.take_along_axis(product[:, j * 128 : (j + 1) * 128], within, axis=1)
            found = jnp.where(tile == i * (step // 128) + j, picked, found)
        return found

    found = lax.fori_loop(
        0, table_ref.shape[0] // step, piece, jnp.zeros((tok, 128), jnp.float32)
    )
    edges_ref[...] = act_ref[...] * found[:, 0:slots]


def body(
    queries,
    keys,
    target_rows,
    target_ids,
    target_weight,
    block_mask,
    value_table,
    feat_shard,
    feat_row,
    activation,
    counts,
):
    tok = queries.shape[0]
    kv_width = keys.shape[1]
    width = kv_width // CHUNKS
    slots = feat_shard.shape[1]
    n = lax.axis_size("seq")
    position = lax.axis_index("seq")
    table = lax.all_gather(value_table, "seq", axis=0, tiled=True)
    live = jnp.arange(slots)[None, :] < counts[:, None]
    act = jnp.where(live, activation, 0.0)

    core = position % 2
    distances = [jnp.zeros_like(position)]
    distances += [jnp.full_like(position, 2 * d) for d in range(1, REACH + 1)]
    distances += [2 * d - 1 + 2 * core for d in range(1, REACH + 1)]
    distances += [7 - 6 * core]
    distance = jnp.stack(distances)
    kept = jnp.sum(
        jnp.where(distance[:, None] - 1 == jnp.arange(WB - 1)[None, :], block_mask, 0), axis=1
    )
    kept = (kept == 1) & (position >= distance)
    mask = jnp.broadcast_to(kept[:, None], (ROLES, GROUP * tok)).astype(jnp.float32)

    vmem = pl.BlockSpec(memory_space=pltpu.VMEM)
    hbm = pl.BlockSpec(memory_space=pl.ANY)
    value_grad = pl.pallas_call(
        functools.partial(attention_kernel, n),
        out_shape=jax.ShapeDtypeStruct((tok, kv_width), jnp.bfloat16),
        in_specs=[hbm, vmem, hbm, vmem, vmem, vmem],
        out_specs=vmem,
        scratch_shapes=[
            pltpu.VMEM(queries.shape, jnp.bfloat16),
            pltpu.VMEM(target_rows.shape, jnp.bfloat16),
            pltpu.VMEM((ROLES - 1, CHUNKS, tok, width), jnp.bfloat16),
            pltpu.VMEM((KVH, GROUP * tok, HD), jnp.bfloat16),
            pltpu.VMEM((ROLES, tok, GROUP * tok), jnp.float32),
            pltpu.VMEM((CHUNKS, tok, width), jnp.float32),
            pltpu.VMEM((REACH, CHUNKS, tok, width), jnp.float32),
            pltpu.VMEM((REACH + 1, CHUNKS, tok, width), jnp.bfloat16),
            pltpu.VMEM((REACH, CHUNKS, tok, width), jnp.bfloat16),
            pltpu.VMEM((REACH, CHUNKS, tok, width), jnp.bfloat16),
            pltpu.VMEM((REACH + 1, CHUNKS, tok, width), jnp.bfloat16),
            pltpu.SemaphoreType.DMA((2,)),
            pltpu.SemaphoreType.DMA((ROLES - 1, CHUNKS)),
            pltpu.SemaphoreType.DMA((ROLES - 1, CHUNKS)),
            pltpu.SemaphoreType.DMA((ROLES - 1, CHUNKS)),
            pltpu.SemaphoreType.DMA((ROLES - 1, CHUNKS)),
        ],
        compiler_params=pltpu.CompilerParams(
            collective_id=0, has_side_effects=True, vmem_limit_bytes=VMEM_LIMIT
        ),
        cost_estimate=pl.CostEstimate(
            flops=2_000_000_000, bytes_accessed=100_000_000, transcendentals=4_000_000
        ),
        name="attention",
    )(queries, keys, target_rows, target_ids, target_weight, mask)

    return pl.pallas_call(
        edges_kernel,
        out_shape=(
            jax.ShapeDtypeStruct((tok, kv_width), jnp.bfloat16),
            jax.ShapeDtypeStruct((tok, slots), jnp.float32),
        ),
        in_specs=[vmem] * 5,
        out_specs=(vmem, vmem),
        scratch_shapes=[pltpu.VMEM((tok, 128), jnp.int32)],
        compiler_params=pltpu.CompilerParams(vmem_limit_bytes=VMEM_LIMIT),
        name="edges",
    )(value_grad, table, feat_shard, feat_row, act)


def solution(mesh):
    tokens = P(("groups", "seq"), None)
    in_specs = (
        tokens,
        tokens,
        P(),
        tokens,
        tokens,
        tokens,
        P("seq", None),
        tokens,
        tokens,
        tokens,
        P(("groups", "seq")),
    )
    return jax.shard_map(
        body, mesh=mesh, in_specs=in_specs, out_specs=(tokens, tokens), check_vma=False
    )
```

time: 219 us -> 92.3 us (0.42); the launches traced: 215 us -> 91.8 us
  waiting for transfers between devices: 89.9 us -> 0.7 us
  Pallas kernels: 0 us -> 66.2 us
  local copies, waits for them, and re-layouts: 50.9 us -> 9.93 us
  starting transfers between devices: 38.3 us -> 0.04 us
  other arithmetic: 9.99 us -> 0.94 us
  matrix products: 7.5 us -> 0 us
  between operations: 18.7 us -> 14.1 us
    ppermute x14 -> x0, waiting for transfers between devices: 89.2 us -> none  [shifted(): return lax.ppermute(block, axis, route)]
    pallas_call x0 -> x2, Pallas kernels: none -> 66.2 us  [the longest x1 64.1 us: body(): pl.pallas_call(functools.partial(attention_kernel, n), out_shape=jax.Shap...]
    ppermute x14 -> x0, starting transfers between devices: 38.3 us -> none  [shifted(): return lax.ppermute(block, axis, route)]
    cond x7 -> x0, local copies, waits for them, and re-layouts: 13.3 us -> none  [body(): lax.cond(allowed[distance], partial_grad, lambda weights: jnp.zeros((tok_...]
    gather x6 -> x0, local copies, waits for them, and re-layouts: 12.3 us -> none  [the longest x5 8.91 us: body(): jnp.take_along_axis(product, jnp.clip(feature, 0, extent - 1), axis=1)]
    another operation x14 -> x1, local copies, waits for them, and re-layouts: 11.9 us -> 0.09 us  [body(): distance = jnp.stack(distances)]
    unnamed x25 -> x15, local copies, waits for them, and re-layouts: 1.21 us -> 9.11 us
    dot_general x3 -> x0, matrix products: 7.5 us -> none  [the longest x1 2.54 us: partial_grad(): jnp.einsum('hgqk,qhgd->khd', pattern, head_grads, preferred_element_type=...]
  transfers between devices with their start and end apart: 15 -> 1, of which waited for: 5 -> 0; matrix products, arithmetic and copies ran while one was open for 26% -> 5% of each run, Pallas kernels for 0% -> 70%
where the time goes in v1:
time: 92.3 us; the launch traced here: 91.8 us
  Pallas kernels  66.2 us (72%)
  between operations  14.1 us (15%)
  local copies, waits for them, and re-layouts  9.93 us (11%)
  other arithmetic  0.94 us (1%)
    pallas_call x1, Pallas kernels, body(): pl.pallas_call(functools.partial(attention_kernel, n), out_shape=jax.Shap...  64.1 us
    unnamed x15, local copies, waits for them, and re-layouts  9.11 us
    pallas_call x1, Pallas kernels, body(): pl.pallas_call(edges_kernel, out_shape=(jax.ShapeDtypeStruct((tok, kv_wid...  2.05 us
  transfers between devices with their start and end apart: 1, of which 0 were waited for; matrix products, arithmetic and copies ran while one was open for 5% of the time, Pallas kernels for 70%

profile of v1, /device:TPU:4, one launch (start us, length us, event | category | flops | bytes accessed | tf_op | source)
XLA Modules:
  0.0 91.8 jit_solution(16928327047910065029)
XLA Ops:
  7.2 0.0 all-gather.2.cloned.1.call-start
  7.2 0.7 all-gather.2.cloned.1.call-update
  7.9 0.8 copy.19.ids_ref
  8.7 0.8 copy.20.weight_ref
  9.5 0.8 copy.22.shard_ref
  10.3 0.8 copy.23.row_ref
  11.1 0.8 copy.21
  11.8 0.1 stack.19
  11.9 0.8 select_reduce_fusion
  12.8 0.1 broadcast_in_dim.31.mask_ref
  12.9 0.0 copy-start.1
  12.9 1.6 %copy-done.1 = bf16[512,2048]{1,0:T(8,128)(2,1)S(1)} copy-done((bf16[512,2048]{1,0:T(8,128)(2,1)S(1)}, bf16[512,2048]{1,0:T(8,128)(2,1)}, u32[]{:S(2)}) %copy-start.1) | copy-done | bytes 2097176
  14.5 0.0 copy-start.2
  14.5 1.0 %copy-done.2 = bf16[128,2048]{1,0:T(8,128)(2,1)S(1)} copy-done((bf16[128,2048]{1,0:T(8,128)(2,1)S(1)}, bf16[128,2048]{1,0:T(8,128)(2,1)}, u32[]{:S(2)}) %copy-start.2) | copy-done | bytes 524312
  15.5 0.0 copy-start.3
  15.5 0.9 %copy-done.3 = bf16[128,1024]{1,0:T(8,128)(2,1)S(1)} copy-done((bf16[128,1024]{1,0:T(8,128)(2,1)S(1)}, bf16[128,1024]{1,0:T(8,128)(2,1)}, u32[]{:S(2)}) %copy-start.3) | copy-done | bytes 262168
  16.4 0.0 copy-start.4
  16.5 64.1 %attention.1.vg_ref = bf16[128,1024]{1,0:T(8,128)(2,1)S(1)} custom-call(bf16[128,2048]{1,0:T(8,128)(2,1)S(1)} %copy-done.2, bf16[128,1024]{1,0:T(8,128)(2,1)S(1)} %copy-done.3, bf16[512,2048]{1,0:T(8,128)(2,1)S(1)} %copy-done.1, s32[128,4]{1,0:T(8,128)S(1)} %copy.19.ids_ref, f32[128,4]{1,0:T(8,128)S(1)} %copy.20.weight_ref, ...), custom_call_target="tpu_custom_call" | custom-call | flops 2000000000 | bytes 100000000 | tf_op jit(solution)/shard_map/attention/pallas_call | solution.py:331
  80.6 0.0 copy-done.4
  80.6 0.1 fusion.act_ref
  80.7 0.0 all-gather.2.cloned.1.call-done.table_ref
  80.7 0.0 copy-start
  80.7 1.6 %copy-done = bf16[1024,1024]{1,0:T(8,128)(2,1)S(1)} copy-done((bf16[1024,1024]{1,0:T(8,128)(2,1)S(1)}, bf16[1024,1024]{1,0:T(8,128)(2,1)}, u32[]{:S(2)}) %copy-start) | copy-done | bytes 2097176
  82.3 2.0 %edges.1 = (bf16[128,1024]{1,0:T(8,128)(2,1)}, f32[128,8]{1,0:T(8,128)S(1)}) custom-call(bf16[128,1024]{1,0:T(8,128)(2,1)S(1)} %attention.1.vg_ref, bf16[1024,1024]{1,0:T(8,128)(2,1)S(1)} %copy-done, s32[128,8]{1,0:T(8,128)S(1)} %copy.22.shard_ref, s32[128,8]{1,0:T(8,128)S(1)} %copy.23.row_ref, f32[128,8]{1,0:T(8,128)S(1)} %fusion.act_ref), custom_call_target="tpu_custom_call" | custom-call | tf_op jit(solution)/shard_map/edges/pallas_call | solution.py:363
  84.3 0.7 copy.24
  (2 shorter events, 0.0 us)
Async XLA Ops:
  7.2 73.5 %all-gather.2.cloned.1.call-start = ((), (), s32[]{:S(2)}) async-start(), calls=%async_computation | async-start | bytes 2228224 | tf_op jit(solution)/shard_map/all_gather | solution.py:313
  12.9 1.6 %copy-start.1 = (bf16[512,2048]{1,0:T(8,128)(2,1)S(1)}, bf16[512,2048]{1,0:T(8,128)(2,1)}, u32[]{:S(2)}) copy-start(bf16[512,2048]{1,0:T(8,128)(2,1)} %rows_hbm.1) | copy-start | bytes 6291460
  14.5 1.0 %copy-start.2 = (bf16[128,2048]{1,0:T(8,128)(2,1)S(1)}, bf16[128,2048]{1,0:T(8,128)(2,1)}, u32[]{:S(2)}) copy-start(bf16[128,2048]{1,0:T(8,128)(2,1)} %q_hbm.1) | copy-start | bytes 1572868
  15.5 0.9 %copy-start.3 = (bf16[128,1024]{1,0:T(8,128)(2,1)S(1)}, bf16[128,1024]{1,0:T(8,128)(2,1)}, u32[]{:S(2)}) copy-start(bf16[128,1024]{1,0:T(8,128)(2,1)} %k_ref.1) | copy-start | bytes 786436
  16.4 64.1 %copy-start.4 = (s32[128]{0:T(128)S(1)}, s32[128]{0:T(128)}, u32[]{:S(2)}) copy-start(s32[128]{0:T(128)} %param.21) | copy-start | bytes 1540
  80.7 1.6 %copy-start = (bf16[1024,1024]{1,0:T(8,128)(2,1)S(1)}, bf16[1024,1024]{1,0:T(8,128)(2,1)}, u32[]{:S(2)}) copy-start(bf16[1024,1024]{1,0:T(8,128)(2,1)} %all-gather.2.cloned.1.call-done.table_ref) | copy-start | bytes 6291460
Sparse Core Ops, SparseCore 0:
  10.2 45.5 all-gather.1

commit v2 on v1

--- a/solution.py
+++ b/solution.py
@@ -22,7 +22,7 @@
 REACH = (WB - 2) // 2
 ROLES = WB
 MESH = pl.DeviceIdType.MESH
-VMEM_LIMIT = 48 * 1024 * 1024
+VMEM_LIMIT = 60 * 1024 * 1024
 
 
 def attention_kernel(
@@ -32,8 +32,16 @@
     rows_hbm,
     ids_ref,
     weight_ref,
+    blocks_ref,
+    table_hbm,
+    shard_ref,
+    row_ref,
+    act_ref,
+    counts_ref,
+    out_ref,
+    edges_ref,
     mask_ref,
-    out_ref,
+    table_vm,
     q_vm,
     rows_vm,
     kbuf,
@@ -50,6 +58,8 @@
     krecv,
     gsend,
     grecv,
+    tsend,
+    trecv,
 ):
     tok = k_ref.shape[0]
     width = k_ref.shape[1] // CHUNKS
@@ -67,6 +77,17 @@
     far = b - 7 + 14 * core
     has_far = jnp.logical_and(far >= 0, far < n)
 
+    group = lax.axis_index("groups")
+    lines = n // 4
+    hi = lax.div(b, 4)
+    lo = lax.rem(chip, 2)
+    mine = core * 2 + lo
+    half = table_hbm.shape[0] // 2
+    part = pl.ds(pl.multiple_of(group * half, half), half)
+    load_table = pltpu.make_async_copy(
+        table_hbm.at[part], table_vm.at[mine, hi, part], load_sem.at[2]
+    )
+    load_table.start()
     load_q = pltpu.make_async_copy(q_hbm, q_vm, load_sem.at[0])
     load_rows = pltpu.make_async_copy(rows_hbm, rows_vm, load_sem.at[1])
     load_rows.start()
@@ -74,19 +95,26 @@
 
     barrier = pltpu.get_barrier_semaphore()
     partners = [(sib, None), (far, has_far)]
-    for d in range(1, REACH + 1):
+    for d in (1, 3):
         partners.append((b + 2 * d, ahead[d - 1]))
         partners.append((b - 2 * d, behind[d - 1]))
 
     def greet(device):
         pl.semaphore_signal(barrier, inc=1, device_id={"seq": device}, device_id_type=MESH)
+
+    def on_line(o):
+        return 4 * lax.rem(hi + o, lines) + 2 * lo + core
+
+    for o in range(1, lines):
+        greet(on_line(o))
+    pl.semaphore_signal(barrier, inc=1, device_id={"groups": 1 - group}, device_id_type=MESH)
 
     for device, cond in partners:
         if cond is None:
             greet(device)
         else:
             pl.when(cond)(functools.partial(greet, device))
-    peers = 1
+    peers = 1 + lines
     for _, cond in partners[1:]:
         peers = peers + jnp.where(cond, 1, 0)
     pl.semaphore_wait(barrier, peers)
@@ -132,36 +160,82 @@
             psend.at[REACH, k], rgrad.at[REACH, k], gsend.at[i, k], grecv.at[i, k], device
         )
 
+    def table_line(o):
+        piece = table_vm.at[mine, hi, part]
+        return remote(piece, piece, tsend.at[o - 1], trecv.at[o - 1], on_line(o))
+
+    def table_lo():
+        piece = table_vm.at[mine, :, part]
+        i = lines - 1
+        return remote(piece, piece, tsend.at[i], trecv.at[i], b + 2 - 4 * lo)
+
+    def table_group():
+        piece = table_vm.at[pl.ds(core * 2, 2), :, part]
+        i = lines
+        return pltpu.make_async_remote_copy(
+            src_ref=piece,
+            dst_ref=piece,
+            send_sem=tsend.at[i],
+            recv_sem=trecv.at[i],
+            device_id={"groups": 1 - group},
+            device_id_type=MESH,
+        )
+
+    def table_core():
+        piece = table_vm.at[pl.ds(core * 2, 2)]
+        i = lines + 1
+        return remote(piece, piece, tsend.at[i], trecv.at[i], sib)
+
     for k in range(CHUNKS):
         for d in range(1, REACH + 1):
             pl.when(ahead[d - 1])(lambda d=d, k=k: key_direct(d, k, b + 2 * d).start())
         pl.when(last_ahead)(lambda k=k: key_last(k, last_key_to).start())
 
+    load_table.wait()
+    for o in range(1, lines):
+        table_line(o).start()
+
     load_rows.wait()
     targets = rows_vm.shape[0]
-    lane = lax.broadcasted_iota(jnp.int32, (tok, targets), 1)
-    spread = jnp.zeros((tok, targets), jnp.float32)
-    for j in range(ids_ref.shape[1]):
-        spread = spread + jnp.where(lane == ids_ref[:, j : j + 1], weight_ref[:, j : j + 1], 0.0)
+    target = lax.broadcasted_iota(jnp.int32, (targets, tok), 0)
+    spread = jnp.zeros((targets, tok), jnp.float32)
+    for j in range(ids_ref.shape[0]):
+        spread = spread + jnp.where(target == ids_ref[j : j + 1, :], weight_ref[j : j + 1, :], 0.0)
+    spread = spread.T
     high = spread.astype(jnp.bfloat16)
     low = (spread - high.astype(jnp.float32)).astype(jnp.bfloat16)
     for g in range(KVH):
-        part = rows_vm[:, g * GROUP * HD : (g + 1) * GROUP * HD]
-        grad = jnp.dot(high, part, preferred_element_type=jnp.float32) + jnp.dot(
-            low, part, preferred_element_type=jnp.float32
+        columns = rows_vm[:, g * GROUP * HD : (g + 1) * GROUP * HD]
+        grad = jnp.dot(high, columns, preferred_element_type=jnp.float32) + jnp.dot(
+            low, columns, preferred_element_type=jnp.float32
         )
         grad = grad.astype(jnp.bfloat16)
         for h in range(GROUP):
             hgrad[g, h * tok : (h + 1) * tok, :] = grad[:, h * HD : (h + 1) * HD]
     load_q.wait()
 
+    def keeps(distance):
+        return blocks_ref[0:1, distance - 1 : distance]
+
+    for r in range(1, ROLES):
+        if r <= REACH:
+            kept, there = keeps(2 * r), behind[r - 1]
+        elif r <= 2 * REACH:
+            d = r - REACH
+            kept = jnp.where(core == 0, keeps(2 * d - 1), keeps(2 * d + 1))
+            there = behind[d - 1]
+        else:
+            kept, there = jnp.where(core == 0, keeps(WB - 1), keeps(1)), last_behind
+        kept = jnp.where(there, kept, 0).astype(jnp.float32)
+        mask_ref[r : r + 1, :] = jnp.broadcast_to(kept, (1, GROUP * tok))
+
     key_row = lax.broadcasted_iota(jnp.int32, (tok, GROUP * tok), 0)
     tok_col = lax.rem(lax.broadcasted_iota(jnp.int32, (tok, GROUP * tok), 1), tok)
     causal = key_row <= tok_col
 
     def tile_work(k):
         for gi in range(HEADS):
-            mine = slice(gi * HD, (gi + 1) * HD)
+            head = slice(gi * HD, (gi + 1) * HD)
             pair = GROUP * HD
             offset = pl.multiple_of(k * (HEADS * pair) + gi * pair, pair)
             q = q_vm[:, pl.ds(offset, pair)]
@@ -173,7 +247,7 @@
                     key = k_ref[:, pl.ds(start, HD)]
                     keep = causal
                 else:
-                    key = kbuf[r - 1, k, :, mine]
+                    key = kbuf[r - 1, k, :, head]
                     keep = mask_ref[r : r + 1, :] > 0.5
                 score = lax.dot_general(
                     key, q2, (((1,), (1,)), ((), ())), preferred_element_type=jnp.float32
@@ -188,13 +262,13 @@
             grad = hgrad[k * HEADS + gi]
             for r in range(ROLES):
                 pattern = (wbuf[r] * scale).astype(jnp.bfloat16)
-                part = jnp.dot(pattern, grad, preferred_element_type=jnp.float32)
+                grads = jnp.dot(pattern, grad, preferred_element_type=jnp.float32)
                 if r == 0:
-                    acc[k, :, mine] = part
+                    acc[k, :, head] = grads
                 elif r <= REACH:
-                    pown[r - 1, k, :, mine] = part
+                    pown[r - 1, k, :, head] = grads
                 else:
-                    psend[r - 1 - REACH, k, :, mine] = part.astype(jnp.bfloat16)
+                    psend[r - 1 - REACH, k, :, head] = grads.astype(jnp.bfloat16)
 
     def reduce_pair(k):
         for d in range(1, REACH + 1):
@@ -223,6 +297,23 @@
             pl.when(behind[d - 1])(lambda d=d: grad_share(d, k).start())
         pl.when(last_behind)(lambda: grad_last(k, last_grad_to).start())
         pl.when(k > 0)(lambda: reduce_pair(k - 1))
+
+        def table_first():
+            for o in range(1, lines):
+                table_line(o).wait_recv()
+            table_lo().start()
+
+        def table_second():
+            table_lo().wait_recv()
+            table_group().start()
+
+        def table_third():
+            table_group().wait_recv()
+            table_core().start()
+
+        pl.when(k == 0)(table_first)
+        pl.when(k == 1)(table_second)
+        pl.when(k == CHUNKS - 1)(table_third)
         return carry
 
     lax.fori_loop(0, CHUNKS, chunk, 0)
@@ -264,31 +355,41 @@
     lax.fori_loop(0, CHUNKS, drain, 0)
 
 
-def edges_kernel(vg_ref, table_ref, shard_ref, row_ref, act_ref, vg_out, edges_ref, wide):
-    tok, slots = shard_ref.shape
-    vg = vg_ref[...]
-    vg_out[...] = vg
-    wide[...] = jnp.zeros_like(wide)
-    wide[:, 0:slots] = shard_ref[...] * FEAT_DEV + row_ref[...]
-    feature = wide[...]
-    tile = lax.div(feature, 128)
-    within = lax.rem(feature, 128)
-    step = 256
-
-    def piece(i, found):
-        rows = table_ref[pl.ds(pl.multiple_of(i * step, step), step), :]
+    table_core().wait_recv()
+    shard = shard_ref[...]
+    slot = (lax.rem(shard, 2) * 2 + lax.rem(lax.div(shard, 2), 2)) * lines + lax.div(shard, 4)
+    depth = table_vm.shape[2]
+    feature = slot * depth + row_ref[...]
+    slots = feature.shape[0]
+    some = math.gcd(lines, 4)
+    step = some * depth
+    place = lax.broadcasted_iota(jnp.int32, (step, tok), 0)
+    vg = out_ref[...]
+
+    def edge_step(i, found):
+        per = lines // some
+        rows = table_vm[lax.div(i, per), pl.ds(lax.rem(i, per) * some, some)].reshape(step, -1)
         product = lax.dot_general(
-            vg, rows, (((1,), (1,)), ((), ())), preferred_element_type=jnp.float32
-        )
-        for j in range(step // 128):
-            picked = jnp.take_along_axis(product[:, j * 128 : (j + 1) * 128], within, axis=1)
-            found = jnp.where(tile == i * (step // 128) + j, picked, found)
-        return found
+            rows, vg, (((1,), (1,)), ((), ())), preferred_element_type=jnp.float32
+        )
+        local = feature - i * step
+        picked = [
+            jnp.sum(jnp.where(place == local[a : a + 1, :], product, 0.0), axis=0, keepdims=True)
+            for a in range(slots)
+        ]
+        return found + jnp.concatenate(picked, axis=0)
 
     found = lax.fori_loop(
-        0, table_ref.shape[0] // step, piece, jnp.zeros((tok, 128), jnp.float32)
+        0, 4 * lines // some, edge_step, jnp.zeros((slots, tok), jnp.float32)
     )
-    edges_ref[...] = act_ref[...] * found[:, 0:slots]
+    live = lax.broadcasted_iota(jnp.int32, (slots, tok), 0) < counts_ref[...]
+    edges_ref[...] = jnp.where(live, act_ref[...] * found, 0.0)
+
+    for o in range(1, lines):
+        table_line(o).wait_send()
+    table_lo().wait_send()
+    table_group().wait_send()
+    table_core().wait_send()
 
 
 def body(
@@ -309,31 +410,21 @@
     width = kv_width // CHUNKS
     slots = feat_shard.shape[1]
     n = lax.axis_size("seq")
-    position = lax.axis_index("seq")
-    table = lax.all_gather(value_table, "seq", axis=0, tiled=True)
-    live = jnp.arange(slots)[None, :] < counts[:, None]
-    act = jnp.where(live, activation, 0.0)
-
-    core = position % 2
-    distances = [jnp.zeros_like(position)]
-    distances += [jnp.full_like(position, 2 * d) for d in range(1, REACH + 1)]
-    distances += [2 * d - 1 + 2 * core for d in range(1, REACH + 1)]
-    distances += [7 - 6 * core]
-    distance = jnp.stack(distances)
-    kept = jnp.sum(
-        jnp.where(distance[:, None] - 1 == jnp.arange(WB - 1)[None, :], block_mask, 0), axis=1
-    )
-    kept = (kept == 1) & (position >= distance)
-    mask = jnp.broadcast_to(kept[:, None], (ROLES, GROUP * tok)).astype(jnp.float32)
+    lines = n // 4
 
     vmem = pl.BlockSpec(memory_space=pltpu.VMEM)
     hbm = pl.BlockSpec(memory_space=pl.ANY)
-    value_grad = pl.pallas_call(
+    value_grad, edges = pl.pallas_call(
         functools.partial(attention_kernel, n),
-        out_shape=jax.ShapeDtypeStruct((tok, kv_width), jnp.bfloat16),
-        in_specs=[hbm, vmem, hbm, vmem, vmem, vmem],
-        out_specs=vmem,
+        out_shape=(
+            jax.ShapeDtypeStruct((tok, kv_width), jnp.bfloat16),
+            jax.ShapeDtypeStruct((slots, tok), jnp.float32),
+        ),
+        in_specs=[hbm, vmem, hbm, vmem, vmem, vmem, hbm, vmem, vmem, vmem, vmem],
+        out_specs=(vmem, vmem),
         scratch_shapes=[
+            pltpu.VMEM((ROLES, GROUP * tok), jnp.float32),
+            pltpu.VMEM((4, lines) + value_table.shape, jnp.bfloat16),
             pltpu.VMEM(queries.shape, jnp.bfloat16),
             pltpu.VMEM(target_rows.shape, jnp.bfloat16),
             pltpu.VMEM((ROLES - 1, CHUNKS, tok, width), jnp.bfloat16),
@@ -345,11 +436,13 @@
             pltpu.VMEM((REACH, CHUNKS, tok, width), jnp.bfloat16),
             pltpu.VMEM((REACH, CHUNKS, tok, width), jnp.bfloat16),
             pltpu.VMEM((REACH + 1, CHUNKS, tok, width), jnp.bfloat16),
-            pltpu.SemaphoreType.DMA((2,)),
+            pltpu.SemaphoreType.DMA((3,)),
             pltpu.SemaphoreType.DMA((ROLES - 1, CHUNKS)),
             pltpu.SemaphoreType.DMA((ROLES - 1, CHUNKS)),
             pltpu.SemaphoreType.DMA((ROLES - 1, CHUNKS)),
             pltpu.SemaphoreType.DMA((ROLES - 1, CHUNKS)),
+            pltpu.SemaphoreType.DMA((lines + 2,)),
+            pltpu.SemaphoreType.DMA((lines + 2,)),
         ],
         compiler_params=pltpu.CompilerParams(
             collective_id=0, has_side_effects=True, vmem_limit_bytes=VMEM_LIMIT
@@ -358,20 +451,20 @@
             flops=2_000_000_000, bytes_accessed=100_000_000, transcendentals=4_000_000
         ),
         name="attention",
-    )(queries, keys, target_rows, target_ids, target_weight, mask)
-
-    return pl.pallas_call(
-        edges_kernel,
-        out_shape=(
-            jax.ShapeDtypeStruct((tok, kv_width), jnp.bfloat16),
-            jax.ShapeDtypeStruct((tok, slots), jnp.float32),
-        ),
-        in_specs=[vmem] * 5,
-        out_specs=(vmem, vmem),
-        scratch_shapes=[pltpu.VMEM((tok, 128), jnp.int32)],
-        compiler_params=pltpu.CompilerParams(vmem_limit_bytes=VMEM_LIMIT),
-        name="edges",
-    )(value_grad, table, feat_shard, feat_row, act)
+    )(
+        queries,
+        keys,
+        target_rows,
+        target_ids.T,
+        target_weight.T,
+        block_mask,
+        value_table,
+        feat_shard.T,
+        feat_row.T,
+        activation.T,
+        counts[None, :],
+    )
+    return value_grad, edges.T
 
 
 def solution(mesh):

time: 92.3 us -> 76.2 us (0.83)
  between operations: 14.1 us -> 0.64 us
  local copies, waits for them, and re-layouts: 9.93 us -> 2.95 us
  Pallas kernels: 66.2 us -> 72.4 us
  other arithmetic: 0.94 us -> 0 us
    pallas_call x2 -> x1, Pallas kernels: 66.2 us -> 72.4 us  [body(): pl.pallas_call(functools.partial(attention_kernel, n), out_shape=(jax.Sha...]
    unnamed x15 -> x2, local copies, waits for them, and re-layouts: 9.11 us -> 2.95 us
  transfers between devices with their start and end apart: 1 -> 0, of which waited for: 0 -> 0; matrix products, arithmetic and copies ran while one was open for 5% -> 0% of each run, Pallas kernels for 70% -> 0%
where the time goes in v2:
time: 76.2 us; the launch traced here: 76 us
  Pallas kernels  72.4 us (95%)
  local copies, waits for them, and re-layouts  2.95 us (4%)
    pallas_call x1, Pallas kernels, body(): pl.pallas_call(functools.partial(attention_kernel, n), out_shape=(jax.Sha...  72.4 us
    unnamed x2, local copies, waits for them, and re-layouts  2.95 us

profile of v2, /device:TPU:4, one launch (start us, length us, event | category | flops | bytes accessed | tf_op | source)
XLA Modules:
  0.0 76.0 jit_solution(9266903450696061471)
XLA Ops:
  0.6 72.4 %attention.1 = (bf16[128,1024]{1,0:T(8,128)(2,1)}, f32[8,128]{1,0:T(8,128)}) custom-call(bf16[128,2048]{1,0:T(8,128)(2,1)} %q_hbm.1, bf16[128,1024]{1,0:T(8,128)(2,1)} %k_ref.1, bf16[512,2048]{1,0:T(8,128)(2,1)} %rows_hbm.1, s32[4,128]{1,0:T(4,128)} %bitcast.11, f32[4,128]{1,0:T(4,128)} %bitcast.12, s32[1,7]{1,0:T(1,128)} %blocks_ref.1, ...), custom_call_target="tpu_custom_call" | custom-call | flops 2000000000 | bytes 100000000 | tf_op jit(solution)/shard_map/attention/pallas_call | solution.py:417
  73.0 1.7 %copy.15 = bf16[128,1024]{1,0:T(8,128)(2,1)} copy(bf16[128,1024]{1,0:T(8,128)(2,1)} %get-tuple-element.8) | data formatting | bytes 524288
  74.7 1.3 %copy.16 = f32[128,8]{0,1:T(8,128)} copy(f32[128,8]{0,1:T(8,128)} %bitcast.7) | data formatting | bytes 8192

commit v3 on v2

--- a/solution.py
+++ b/solution.py
@@ -186,14 +186,16 @@
         i = lines + 1
         return remote(piece, piece, tsend.at[i], trecv.at[i], sib)
 
-    for k in range(CHUNKS):
-        for d in range(1, REACH + 1):
-            pl.when(ahead[d - 1])(lambda d=d, k=k: key_direct(d, k, b + 2 * d).start())
-        pl.when(last_ahead)(lambda k=k: key_last(k, last_key_to).start())
+    def send_keys(chunks):
+        for k in chunks:
+            for d in range(1, REACH + 1):
+                pl.when(ahead[d - 1])(lambda d=d, k=k: key_direct(d, k, b + 2 * d).start())
+            pl.when(last_ahead)(lambda k=k: key_last(k, last_key_to).start())
 
     load_table.wait()
     for o in range(1, lines):
         table_line(o).start()
+    send_keys(range(CHUNKS // 2))
 
     load_rows.wait()
     targets = rows_vm.shape[0]
@@ -212,6 +214,10 @@
         grad = grad.astype(jnp.bfloat16)
         for h in range(GROUP):
             hgrad[g, h * tok : (h + 1) * tok, :] = grad[:, h * HD : (h + 1) * HD]
+    for o in range(1, lines):
+        table_line(o).wait_recv()
+    table_lo().start()
+    send_keys(range(CHUNKS // 2, CHUNKS))
     load_q.wait()
 
     def keeps(distance):
@@ -298,22 +304,16 @@
         pl.when(last_behind)(lambda: grad_last(k, last_grad_to).start())
         pl.when(k > 0)(lambda: reduce_pair(k - 1))
 
-        def table_first():
-            for o in range(1, lines):
-                table_line(o).wait_recv()
-            table_lo().start()
-
-        def table_second():
+        def table_cross():
             table_lo().wait_recv()
             table_group().start()
 
-        def table_third():
+        def table_share():
             table_group().wait_recv()
             table_core().start()
 
-        pl.when(k == 0)(table_first)
-        pl.when(k == 1)(table_second)
-        pl.when(k == CHUNKS - 1)(table_third)
+        pl.when(k == 0)(table_cross)
+        pl.when(k == CHUNKS - 1)(table_share)
         return carry
 
     lax.fori_loop(0, CHUNKS, chunk, 0)

time: 76.2 us -> 65 us (0.85)
  Pallas kernels: 72.4 us -> 61.2 us
    pallas_call x1, Pallas kernels: 72.4 us -> 61.2 us  [body(): pl.pallas_call(functools.partial(attention_kernel, n), out_shape=(jax.Sha...]
where the time goes in v3:
time: 65 us; the launch traced here: 64.8 us
  Pallas kernels  61.2 us (94%)
  local copies, waits for them, and re-layouts  2.95 us (5%)
    pallas_call x1, Pallas kernels, body(): pl.pallas_call(functools.partial(attention_kernel, n), out_shape=(jax.Sha...  61.2 us
    unnamed x2, local copies, waits for them, and re-layouts  2.95 us

profile of v3, /device:TPU:4, one launch (start us, length us, event | category | flops | bytes accessed | tf_op | source)
XLA Modules:
  0.0 64.8 jit_solution(4037884195347371723)
XLA Ops:
  0.6 61.2 %attention.1 = (bf16[128,1024]{1,0:T(8,128)(2,1)}, f32[8,128]{1,0:T(8,128)}) custom-call(bf16[128,2048]{1,0:T(8,128)(2,1)} %q_hbm.1, bf16[128,1024]{1,0:T(8,128)(2,1)} %k_ref.1, bf16[512,2048]{1,0:T(8,128)(2,1)} %rows_hbm.1, s32[4,128]{1,0:T(4,128)} %bitcast.11, f32[4,128]{1,0:T(4,128)} %bitcast.12, s32[1,7]{1,0:T(1,128)} %blocks_ref.1, ...), custom_call_target="tpu_custom_call" | custom-call | flops 2000000000 | bytes 100000000 | tf_op jit(solution)/shard_map/attention/pallas_call | solution.py:417
  61.9 1.7 %copy.15 = bf16[128,1024]{1,0:T(8,128)(2,1)} copy(bf16[128,1024]{1,0:T(8,128)(2,1)} %get-tuple-element.8) | data formatting | bytes 524288
  63.5 1.3 %copy.16 = f32[128,8]{0,1:T(8,128)} copy(f32[128,8]{0,1:T(8,128)} %bitcast.7) | data formatting | bytes 8192

commit v4 on v3

--- a/solution.py
+++ b/solution.py
@@ -16,7 +16,7 @@
 FEAT_DEV = 64
 SOFTCAP = 50.0
 
-CHUNKS = 4
+CHUNKS = 8
 GROUP = H // KVH
 HEADS = KVH // CHUNKS
 REACH = (WB - 2) // 2

time: 65 us -> 61.8 us (0.951)
  Pallas kernels: 61.2 us -> 58 us
    pallas_call x1, Pallas kernels: 61.2 us -> 58 us  [body(): pl.pallas_call(functools.partial(attention_kernel, n), out_shape=(jax.Sha...]
where the time goes in v4:
time: 61.8 us; the launch traced here: 61.6 us
  Pallas kernels  58 us (94%)
  local copies, waits for them, and re-layouts  2.95 us (5%)
  between operations  0.64 us (1%)
    pallas_call x1, Pallas kernels, body(): pl.pallas_call(functools.partial(attention_kernel, n), out_shape=(jax.Sha...  58 us
    unnamed x2, local copies, waits for them, and re-layouts  2.95 us

profile of v4, /device:TPU:4, one launch (start us, length us, event | category | flops | bytes accessed | tf_op | source)
XLA Modules:
  0.0 61.6 jit_solution(3861950672119958501)
XLA Ops:
  0.6 58.0 %attention.1 = (bf16[128,1024]{1,0:T(8,128)(2,1)}, f32[8,128]{1,0:T(8,128)}) custom-call(bf16[128,2048]{1,0:T(8,128)(2,1)} %q_hbm.1, bf16[128,1024]{1,0:T(8,128)(2,1)} %k_ref.1, bf16[512,2048]{1,0:T(8,128)(2,1)} %rows_hbm.1, s32[4,128]{1,0:T(4,128)} %bitcast.11, f32[4,128]{1,0:T(4,128)} %bitcast.12, s32[1,7]{1,0:T(1,128)} %blocks_ref.1, ...), custom_call_target="tpu_custom_call" | custom-call | flops 2000000000 | bytes 100000000 | tf_op jit(solution)/shard_map/attention/pallas_call | solution.py:417
  58.7 1.7 %copy.15 = bf16[128,1024]{1,0:T(8,128)(2,1)} copy(bf16[128,1024]{1,0:T(8,128)(2,1)} %get-tuple-element.8) | data formatting | bytes 524288
  60.3 1.3 %copy.16 = f32[128,8]{0,1:T(8,128)} copy(f32[128,8]{0,1:T(8,128)} %bitcast.7) | data formatting | bytes 8192
